TPU v7x, 512 devices: a whole 4x4x16 slice. The times are simulated.
512 devices in a mesh: seg: 16 (over x, z_hi, core), blk: 4 (over y), uly: 8 (over z_lo).
Axes of the slice: x: 4, y: 4, z: 16 (z_hi: 2, z_lo: 8; z = z_hi * 8 + z_lo), core: 2. Of those that a mesh axis runs over, the one named last changes fastest.
Arguments:
- queries: bfloat16 [8192, 5120], P(('seg', 'blk', 'uly')), may hold values from -16 to 16
- keys: bfloat16 [8192, 5120], P(('seg', 'blk', 'uly')), may hold values from -16 to 16
- values: bfloat16 [8192, 5120], P(('seg', 'blk', 'uly')), may hold values from -6 to 6
- gain_q: float32 [5120], replicated, may hold values from 1.2 to 2.2
- gain_k: float32 [5120], replicated, may hold values from 1.2 to 2.2
- positions: int32 [3, 8192], P(None, ('seg', 'blk', 'uly')), may hold values from 0 to 51, as said below
- ref_group: int32 [16], replicated, may hold values from 0 to 15, each once
Outputs:
- attended: bfloat16 [8192, 5120], P(('seg', 'blk', 'uly'))
Inputs may be any that keep to these rules, and one draw needn't show every extreme that they name: `positions`: frame below 21, row below 30, column below 52. `ref_group`: a permutation of the group numbers.
All inputs are finite; a program needn't handle non-finite values.
Results may differ from a plain program's by a relative error of at most 0.0095.
Values may be sent and summed in bfloat16 or wider, within the bound.
No kernel may reach another device: no remote copies, remote signals or barrier semaphores. Data moves between devices by JAX's collectives and lax.ppermute only.
A program may use at most 64 MiB of HBM per device.

v0:
```python
import jax
import jax.numpy as jnp
from jax import lax
from jax.sharding import PartitionSpec as P

HEAD_DIM = 128


def broadcast(shard, axis, root):
    mine = lax.axis_index(axis) == root
    return lax.psum(jnp.where(mine, shard, jnp.zeros_like(shard)), axis)


def norm_rows(source, gain):
    wide = source.astype(jnp.float32)
    mean_square = jnp.mean(wide * wide, axis=-1, keepdims=True)
    return wide * lax.rsqrt(mean_square + 1e-06) * gain


def rope_angles(positions, head_dim):
    pair_count = head_dim // 2
    side_pairs = head_dim // 6
    time_pairs = pair_count - 2 * side_pairs

    def frequencies(number):
        return 1.0 / 10000.0 ** (jnp.arange(number, dtype=jnp.float32) * 2.0 / (2 * number))

    position_f = positions.astype(jnp.float32)
    angles = jnp.concatenate(
        [
            position_f[0][:, None] * frequencies(time_pairs)[None, :],
            position_f[1][:, None] * frequencies(side_pairs)[None, :],
            position_f[2][:, None] * frequencies(side_pairs)[None, :],
        ],
        axis=1,
    )
    return (jnp.cos(angles), jnp.sin(angles))


def rotate(source, cos_table, sin_table, head_count, head_dim):
    token_count = source.shape[0]
    paired = source.reshape(token_count, head_count, head_dim // 2, 2)
    real_part = paired[..., 0]
    imag_part = paired[..., 1]
    cos_b = cos_table[:, None, :]
    sin_b = sin_table[:, None, :]
    turned = jnp.stack(
        [real_part * cos_b - imag_part * sin_b, real_part * sin_b + imag_part * cos_b], axis=-1
    )
    return turned.reshape(token_count, head_count * head_dim)


def absorb(folded, queried, key_rows, value_rows):
    running_max, running_sum, weighted = folded
    key_count = key_rows.shape[0]
    head_count = queried.shape[1]
    key_heads = key_rows.reshape(key_count, head_count, HEAD_DIM)
    value_heads = value_rows.reshape(key_count, head_count, HEAD_DIM)
    score_scale = HEAD_DIM ** (-0.5)
    scores = (
        jnp.einsum("qhd,khd->qhk", queried, key_heads, preferred_element_type=jnp.float32)
        * score_scale
    )
    new_max = jnp.maximum(running_max, jnp.max(scores, axis=2))
    rescale = jnp.exp(running_max - new_max)
    weights = jnp.exp(scores - new_max[..., None])
    running_sum = running_sum * rescale + jnp.sum(weights, axis=2)
    weighted = weighted * rescale[..., None] + jnp.einsum(
        "qhk,khd->qhd",
        weights.astype(jnp.bfloat16),
        value_heads,
        preferred_element_type=jnp.float32,
    )
    return (new_max, running_sum, weighted)


def local(queries, keys, values, gain_q, gain_k, positions, ref_group):
    head_count = queries.shape[1] // HEAD_DIM
    cos_table, sin_table = rope_angles(positions, HEAD_DIM)
    q_rot = rotate(norm_rows(queries, gain_q), cos_table, sin_table, head_count, HEAD_DIM).astype(
        jnp.bfloat16
    )
    k_rot = rotate(norm_rows(keys, gain_k), cos_table, sin_table, head_count, HEAD_DIM).astype(
        jnp.bfloat16
    )
    q_heads, k_heads, v_heads = (
        lax.all_to_all(q_rot, "uly", split_axis=1, concat_axis=0, tiled=True),
        lax.all_to_all(k_rot, "uly", split_axis=1, concat_axis=0, tiled=True),
        lax.all_to_all(values, "uly", split_axis=1, concat_axis=0, tiled=True),
    )
    row_count = q_heads.shape[0]
    local_heads = q_heads.shape[1] // HEAD_DIM
    queried = q_heads.reshape(row_count, local_heads, HEAD_DIM)
    initial = (
        jnp.full((row_count, local_heads), -1e30, jnp.float32),
        jnp.zeros((row_count, local_heads), jnp.float32),
        jnp.zeros((row_count, local_heads, HEAD_DIM), jnp.float32),
    )
    group_ids = jnp.arange(ref_group.shape[0], dtype=jnp.int32)
    ref_root = jnp.sum(jnp.where(ref_group == 0, group_ids, 0))
    ref_keys, ref_values = (
        broadcast(k_heads, "seg", ref_root),
        broadcast(v_heads, "seg", ref_root),
    )
    folded = initial
    folded = absorb(
        folded,
        queried,
        lax.all_gather(k_heads, "blk", axis=0, tiled=True),
        lax.all_gather(v_heads, "blk", axis=0, tiled=True),
    )
    folded = absorb(
        folded,
        queried,
        lax.all_gather(ref_keys, "blk", axis=0, tiled=True),
        lax.all_gather(ref_values, "blk", axis=0, tiled=True),
    )
    running_max, running_sum, weighted = folded
    result = (
        (weighted / running_sum[..., None])
        .reshape(row_count, local_heads * HEAD_DIM)
        .astype(jnp.bfloat16)
    )
    return lax.all_to_all(result, "uly", split_axis=0, concat_axis=1, tiled=True)


def solution(mesh):
    in_specs = (
        P(("seg", "blk", "uly"), None),
        P(("seg", "blk", "uly"), None),
        P(("seg", "blk", "uly"), None),
        P(),
        P(),
        P(None, ("seg", "blk", "uly")),
        P(),
    )
    out_specs = P(("seg", "blk", "uly"), None)
    return jax.shard_map(local, mesh=mesh, in_specs=in_specs, out_specs=out_specs, check_vma=False)
```

profile of v0, /device:TPU:24, one launch (start us, length us, event | category | flops | bytes accessed | tf_op | source)
XLA Modules:
  0.0 393.1 jit_solution(6911439188917561661)
XLA Ops:
  7.7 1.1 fusion.15
  8.8 1.0 fusion.16
  9.8 0.7 copy.76
  11.0 2.2 copy.81
  13.3 8.3 %subtract_convert_fusion = (bf16[16,40,64,1]{0,3,2,1:T(2,128)(2,1)S(1)}, bf16[16,40,64,1]{0,3,2,1:T(2,128)(2,1)S(1)}, bf16[16,40,64,1]{0,3,2,1:T(2,128)(2,1)S(1)}, bf16[16,40,64,1]{0,3,2,1:T(2,128)(2,1)S(1)}) fusion(f32[16,40,64,2]{0,3,2,1:T(2,128)} %bitcast.53, f32[16,64]{0,1:T(8,128)S(1)} %copy.78, f32[16,64]{0,1:T(8,128)S(1)} %copy.77, ...), kind=kLoop, calls=%fused_computation.9 | loop fusion | flops 655360 | bytes 991232 | tf_op jit(solution)/shard_map/convert
  21.6 7.3 %pad_maximum_fusion = (bf16[16,40,64,2]{0,3,2,1:T(2,128)(2,1)S(1)}, bf16[16,40,64,2]{0,3,2,1:T(2,128)(2,1)S(1)}) fusion(bf16[16,40,64,1]{0,3,2,1:T(2,128)(2,1)S(1)} %get-tuple-element.13, bf16[16,40,64,1]{0,3,2,1:T(2,128)(2,1)S(1)} %get-tuple-element.14, bf16[16,40,64,1]{0,3,2,1:T(2,128)(2,1)S(1)} %get-tuple-element.10, ...), kind=kLoop, calls=%fused_computation.4 | loop fusion | flops 655360 | bytes 655360 | tf_op jit(solution)/shard_map/stack | solution.py:47
  28.8 1.0 copy.79
  29.9 12.7 %all-to-all-start = ((bf16[16,8,640]{2,0,1:T(8,128)(2,1)}), bf16[16,8,640]{2,0,1:T(8,128)(2,1)S(1)}, u32[]{:S(2)}, u32[]{:S(2)}) async-start(bf16[16,8,640]{2,0,1:T(8,128)(2,1)} %copy.79), calls=%async_computation | async-start | bytes 327680 | tf_op jit(solution)/shard_map/all_to_all | solution.py:88
  43.2 12.2 %all-to-all-done = bf16[16,8,640]{2,0,1:T(8,128)(2,1)S(1)} async-done(((bf16[16,8,640]{2,0,1:T(8,128)(2,1)}), bf16[16,8,640]{2,0,1:T(8,128)(2,1)S(1)}, u32[]{:S(2)}, u32[]{:S(2)}) %all-to-all-start) | async-done | bytes 163872 | tf_op jit(solution)/shard_map/all_to_all | solution.py:88
  55.4 4.7 %all-to-all-start.2 = ((bf16[16,8,640]{2,0,1:T(8,128)(2,1)}), bf16[16,8,640]{2,0,1:T(8,128)(2,1)S(1)}, u32[]{:S(2)}, u32[]{:S(2)}) async-start(bf16[16,8,640]{2,0,1:T(8,128)(2,1)} %bitcast.51), calls=%async_computation.2 | async-start | bytes 327680 | tf_op jit(solution)/shard_map/all_to_all | solution.py:89
  60.1 1.0 copy.82
  62.4 0.7 broadcast_select_fusion.1
  63.1 10.0 %all-to-all-done.2 = bf16[16,8,640]{2,0,1:T(8,128)(2,1)S(1)} async-done(((bf16[16,8,640]{2,0,1:T(8,128)(2,1)}), bf16[16,8,640]{2,0,1:T(8,128)(2,1)S(1)}, u32[]{:S(2)}, u32[]{:S(2)}) %all-to-all-start.2) | async-done | bytes 163872 | tf_op jit(solution)/shard_map/all_to_all | solution.py:89
  73.1 4.7 %all-to-all-start.1 = ((bf16[16,8,640]{2,0,1:T(8,128)(2,1)}), bf16[16,8,640]{2,0,1:T(8,128)(2,1)S(1)}, u32[]{:S(2)}, u32[]{:S(2)}) async-start(bf16[16,8,640]{2,0,1:T(8,128)(2,1)} %copy.82), calls=%async_computation.1 | async-start | bytes 327680 | tf_op jit(solution)/shard_map/all_to_all | solution.py:87
  77.9 0.7 broadcast_select_fusion
  78.6 13.8 %all_gather.12 = bf16[512,640]{1,0:T(8,128)(2,1)S(1)} all-gather(bf16[128,640]{1,0:T(8,128)(2,1)S(1)} %bitcast.59), channel_id=1, replica_groups=mesh['seg'=16,'blk'=4,'uly'=8] {'blk'}, dimensions={0}, use_global_device_ids=true | all-gather | bytes 819200 | tf_op jit(solution)/shard_map/all_gather | solution.py:109
  92.4 13.5 %all_gather.13 = bf16[512,640]{1,0:T(8,128)(2,1)S(1)} all-gather(bf16[128,640]{1,0:T(8,128)(2,1)S(1)} %bitcast.60), channel_id=1, replica_groups=mesh['seg'=16,'blk'=4,'uly'=8] {'blk'}, dimensions={0}, use_global_device_ids=true | all-gather | bytes 819200 | tf_op jit(solution)/shard_map/all_gather | solution.py:110
  106.3 1.1 copy.86
  107.8 224.8 %all-reduce.3.cloned.1.call-done = (bf16[128,640]{1,0:T(8,128)(2,1)}, bf16[128,640]{1,0:T(8,128)(2,1)}) async-done(((bf16[128,640]{1,0:T(8,128)(2,1)}, bf16[128,640]{1,0:T(8,128)(2,1)}), (bf16[128,640]{1,0:T(8,128)(2,1)}, bf16[128,640]{1,0:T(8,128)(2,1)})) %all-reduce.3.cloned.1.call-update) | async-done | bytes 327696 | tf_op jit(solution)/shard_map/psum | solution.py:11
  332.7 14.1 %all_gather.14 = bf16[512,640]{1,0:T(8,128)(2,1)S(1)} all-gather(bf16[128,640]{1,0:T(8,128)(2,1)} %get-tuple-element.6), channel_id=1, replica_groups=mesh['seg'=16,'blk'=4,'uly'=8] {'blk'}, dimensions={0}, use_global_device_ids=true | all-gather | bytes 819200 | tf_op jit(solution)/shard_map/all_gather | solution.py:115
  347.9 13.9 %all_gather.15 = bf16[512,640]{1,0:T(8,128)(2,1)S(1)} all-gather(bf16[128,640]{1,0:T(8,128)(2,1)S(1)} %copy-done.4), channel_id=1, replica_groups=mesh['seg'=16,'blk'=4,'uly'=8] {'blk'}, dimensions={0}, use_global_device_ids=true | all-gather | bytes 819200 | tf_op jit(solution)/shard_map/all_gather | solution.py:116
  361.8 1.1 copy.92
  363.1 0.9 copy-done
  366.0 19.6 %all_to_all.64 = bf16[8,16,640]{2,1,0:T(8,128)(2,1)S(1)} all-to-all(bf16[8,16,640]{2,1,0:T(8,128)(2,1)S(1)} %convert_element_type.40), channel_id=1, replica_groups=mesh['seg'=16,'blk'=4,'uly'=8] {'uly'}, dimensions={0} | all-to-all | bytes 327680 | tf_op jit(solution)/shard_map/all_to_all | solution.py:124
  (45 shorter events, 7.8 us)
Async XLA Ops:
  9.8 0.9 copy-start.1
  9.8 1.1 copy-start.5
  28.8 13.7 %copy-start.3 = (bf16[16,5120]{1,0:T(8,128)(2,1)S(1)}, bf16[16,5120]{1,0:T(8,128)(2,1)}, u32[]{:S(2)}) copy-start(bf16[16,5120]{1,0:T(8,128)(2,1)} %param.9) | copy-start | bytes 491524
  29.9 31.3 %copy-start.6 = (s32[16]{0:T(128)S(1)}, s32[16]{0:T(128)}, u32[]{:S(2)}) copy-start(s32[16]{0:T(128)} %param.13) | copy-start | bytes 196
  29.9 25.5 %all-to-all-start = ((bf16[16,8,640]{2,0,1:T(8,128)(2,1)}), bf16[16,8,640]{2,0,1:T(8,128)(2,1)S(1)}, u32[]{:S(2)}, u32[]{:S(2)}) async-start(bf16[16,8,640]{2,0,1:T(8,128)(2,1)} %copy.79), calls=%async_computation | async-start | bytes 327680 | tf_op jit(solution)/shard_map/all_to_all | solution.py:88
  55.4 17.7 %all-to-all-start.2 = ((bf16[16,8,640]{2,0,1:T(8,128)(2,1)}), bf16[16,8,640]{2,0,1:T(8,128)(2,1)S(1)}, u32[]{:S(2)}, u32[]{:S(2)}) async-start(bf16[16,8,640]{2,0,1:T(8,128)(2,1)} %bitcast.51), calls=%async_computation.2 | async-start | bytes 327680 | tf_op jit(solution)/shard_map/all_to_all | solution.py:89
  73.1 33.0 %all-to-all-start.1 = ((bf16[16,8,640]{2,0,1:T(8,128)(2,1)}), bf16[16,8,640]{2,0,1:T(8,128)(2,1)S(1)}, u32[]{:S(2)}, u32[]{:S(2)}) async-start(bf16[16,8,640]{2,0,1:T(8,128)(2,1)} %copy.82), calls=%async_computation.1 | async-start | bytes 327680 | tf_op jit(solution)/shard_map/all_to_all | solution.py:87
  77.8 254.8 %all-reduce.3.cloned.1.call-start = ((), (), s32[]{:S(2)}) async-start(), calls=%async_computation.4 | async-start | bytes 655360 | tf_op jit(solution)/shard_map/psum | solution.py:11
  347.0 0.9 copy-start.4
  362.9 1.1 copy-start
  364.0 1.1 copy-start.2
Sparse Core Ops, SparseCore 0:
  81.6 250.9 all-reduce.2
where the time goes:
time: 394 us; the launch traced here: 393 us
  waiting for transfers between devices  247 us (63%)
  blocking collectives  74.8 us (19%)
  starting transfers between devices  22.1 us (6%)
  other arithmetic  21.3 us (5%)
  between operations  14.2 us (4%)
  local copies, waits for them, and re-layouts  11.8 us (3%)
    psum x1, waiting for transfers between devices, broadcast(): return lax.psum(jnp.where(mine, shard, jnp.zeros_like(shard)), axis)  225 us
    all_to_all x1, blocking collectives, local(): lax.all_to_all(result, 'uly', split_axis=0, concat_axis=1, tiled=True)  19.6 us
    all_gather x1, blocking collectives, local(): lax.all_gather(ref_keys, 'blk', axis=0, tiled=True)  14.1 us
    all_gather x1, blocking collectives, local(): lax.all_gather(ref_values, 'blk', axis=0, tiled=True)  13.9 us
    all_gather x1, blocking collectives, local(): lax.all_gather(k_heads, 'blk', axis=0, tiled=True)  13.8 us
    all_gather x1, blocking collectives, local(): lax.all_gather(v_heads, 'blk', axis=0, tiled=True)  13.5 us
    all_to_all x1, starting transfers between devices, local(): lax.all_to_all(k_rot, 'uly', split_axis=1, concat_axis=0, tiled=True)  12.7 us
    all_to_all x1, waiting for transfers between devices, local(): lax.all_to_all(k_rot, 'uly', split_axis=1, concat_axis=0, tiled=True)  12.2 us
  transfers between devices with their start and end apart: 4, of which 3 were waited for; matrix products, arithmetic and copies ran while one was open for 1% of the time, Pallas kernels for 0%

commit v1 on v0

v1 whole, which is shorter than its diff:
```python
import jax
import jax.numpy as jnp
from jax import lax
from jax.experimental import pallas as pl
from jax.experimental.pallas import tpu as pltpu
from jax.sharding import Mesh, PartitionSpec as P

HEADS = 40
HEAD_DIM = 128
WIDTH = HEADS * HEAD_DIM
BLK = 4
ULY = 8
PEERS = BLK * ULY
TOKENS = 16
QUARTER = TOKENS // BLK
COLUMN = 8
ROWS = TOKENS + 8
SHARED_ROW = 3 * TOKENS
REF_ROW = SHARED_ROW + 3 * QUARTER
ALL_SETS = (REF_ROW + 8) // QUARTER
PAIR = 2 * HEAD_DIM
VMEM_LIMIT = 48 * 1024 * 1024
PARAMS = pltpu.CompilerParams(vmem_limit_bytes=VMEM_LIMIT)
WHOLE_VMEM = pltpu.CompilerParams(vmem_limit_bytes=60 * 1024 * 1024)
VMEM = pl.BlockSpec(memory_space=pltpu.VMEM)
ANY = pl.BlockSpec(memory_space=pl.ANY)
HBM = pl.BlockSpec(memory_space=pltpu.HBM)


def lanes(index, width=HEAD_DIM):
    return slice(index * width, (index + 1) * width)


def peers():
    for blk in range(BLK):
        for uly in range(ULY):
            yield blk * ULY + uly, blk, BLK * uly + blk, PEERS + uly


def rotary_tables(position):
    pairs = HEAD_DIM // 2
    side = HEAD_DIM // 6
    time = pairs - 2 * side
    eye = lax.broadcasted_iota(jnp.int32, (TOKENS, TOKENS), 0) == lax.broadcasted_iota(
        jnp.int32, (TOKENS, TOKENS), 1
    )
    columns = [
        jnp.sum(jnp.where(eye, position[axis : axis + 1, :], 0.0), axis=1, keepdims=True)
        for axis in range(3)
    ]
    lane = lax.broadcasted_iota(jnp.int32, (TOKENS, HEAD_DIM), 1)
    pair = lax.shift_right_logical(lane, 1)
    in_time = pair < time
    in_row = pair < time + side
    local = (pair - jnp.where(in_time, 0, jnp.where(in_row, time, time + side))).astype(jnp.float32)
    number = jnp.where(in_time, float(time), float(side))
    frequency = jnp.exp(local / number * -9.210340371976184)
    angle = jnp.where(in_time, columns[0], jnp.where(in_row, columns[1], columns[2])) * frequency
    return jnp.cos(angle), jnp.sin(angle), lax.rem(lane, 2) == 0


def inverse_rms(source_ref):
    wide = source_ref[...].astype(jnp.float32)
    return lax.rsqrt(jnp.mean(wide * wide, axis=1, keepdims=True) + 1e-06)


def rotation(pos_ref):
    cos, sin, even = rotary_tables(pos_ref[...].astype(jnp.float32))
    return cos, jnp.where(even, -sin, 0.0), jnp.where(even, 0.0, sin)


def turn(source_ref, gain_ref, head, scale, tables):
    cos, sin_next, sin_prev = tables
    normed = source_ref[:, lanes(head)].astype(jnp.float32) * scale * gain_ref[:, lanes(head)]
    turned = (
        normed * cos
        + pltpu.roll(normed, HEAD_DIM - 1, 1) * sin_next
        + pltpu.roll(normed, 1, 1) * sin_prev
    )
    return turned.astype(jnp.bfloat16)


def spread(out_ref, head, block, main_row, shared_row):
    for peer, blk, whole, shared in peers():
        if head == whole:
            out_ref[peer, main_row : main_row + TOKENS, :] = block
        if head == shared:
            out_ref[peer, shared_row : shared_row + QUARTER, :] = block[
                QUARTER * blk : QUARTER * (blk + 1), :
            ]


def start_all(pairs, sems):
    copies = [
        pltpu.make_async_copy(source, target, sems.at[index])
        for index, (source, target) in enumerate(pairs)
    ]
    for copy in copies:
        copy.start()
    return copies


WIDE = pltpu.VMEM((TOKENS, WIDTH), jnp.bfloat16)
GAIN = pltpu.VMEM((1, WIDTH), jnp.float32)
PLACES = pltpu.VMEM((3, TOKENS), jnp.int32)


def pieces_kernel(
    k_hbm, v_hbm, gk_hbm, pos_hbm, group_hbm, ref_out, place_out,
    k_ref, v_ref, gk_ref, pos_ref, group_ref, sems,
):
    pairs = [
        (pos_hbm, pos_ref), (k_hbm, k_ref), (gk_hbm, gk_ref),
        (v_hbm, v_ref), (group_hbm, group_ref),
    ]
    copies = start_all(pairs, sems)

    def share(head, block, half):
        for piece in range(COLUMN):
            ref_out[piece, :, lanes(2 * head + half)] = block[2 * piece : 2 * piece + 2, :]

    copies[0].wait()
    tables = rotation(pos_ref)
    copies[1].wait()
    copies[2].wait()
    scale = inverse_rms(k_ref)
    for head in range(HEADS):
        share(head, turn(k_ref, gk_ref, head, scale, tables), 0)
    copies[3].wait()
    for head in range(HEADS):
        share(head, v_ref[:, lanes(head)], 1)
    copies[4].wait()
    group = group_ref[...]
    ids = lax.broadcasted_iota(jnp.int32, group.shape, 1)
    root = jnp.sum(jnp.where(group == 0, ids, 0), axis=1, keepdims=True)
    source = 2 * lax.shift_right_logical(root, 2) + jnp.bitwise_and(root, 1)
    half = jnp.bitwise_and(lax.shift_right_logical(root, 1) + lax.axis_index("half"), 1)
    lane = lax.broadcasted_iota(jnp.int32, place_out.shape, 1)
    place_out[...] = jnp.where(lane == 0, source, half)


def make_pieces(keys, values, gain_k, positions, ref_group):
    return pl.pallas_call(
        pieces_kernel,
        in_specs=[HBM] * 5,
        out_specs=(VMEM,) * 2,
        out_shape=(
            jax.ShapeDtypeStruct((COLUMN, 2, HEADS * PAIR), jnp.bfloat16),
            jax.ShapeDtypeStruct((8, HEAD_DIM), jnp.int32),
        ),
        scratch_shapes=[
            WIDE, WIDE, GAIN, PLACES,
            pltpu.VMEM((1, 16), jnp.int32),
            pltpu.SemaphoreType.DMA((5,)),
        ],
        compiler_params=WHOLE_VMEM,
        name="reference_pieces",
    )(keys, values, gain_k.reshape(1, WIDTH), positions, ref_group.reshape(1, 16))


def blocks_kernel(
    q_hbm, k_hbm, v_hbm, gq_hbm, gk_hbm, pos_hbm, out_ref,
    q_ref, k_ref, v_ref, gq_ref, gk_ref, pos_ref, sems,
):
    pairs = [
        (pos_hbm, pos_ref), (k_hbm, k_ref), (gk_hbm, gk_ref),
        (v_hbm, v_ref), (q_hbm, q_ref), (gq_hbm, gq_ref),
    ]
    copies = start_all(pairs, sems)

    def place(head, block, part):
        spread(out_ref, head, block, TOKENS * part, SHARED_ROW + QUARTER * part)

    copies[0].wait()
    tables = rotation(pos_ref)
    copies[1].wait()
    copies[2].wait()
    scale = inverse_rms(k_ref)
    for head in range(HEADS):
        place(head, turn(k_ref, gk_ref, head, scale, tables), 0)
    copies[3].wait()
    for head in range(HEADS):
        place(head, v_ref[:, lanes(head)], 1)
    copies[4].wait()
    copies[5].wait()
    scale = inverse_rms(q_ref)
    for head in range(HEADS):
        place(head, turn(q_ref, gq_ref, head, scale, tables), 2)


def make_blocks(queries, keys, values, gain_q, gain_k, positions):
    return pl.pallas_call(
        blocks_kernel,
        in_specs=[HBM] * 6,
        out_specs=VMEM,
        out_shape=jax.ShapeDtypeStruct((PEERS, REF_ROW + 4, HEAD_DIM), jnp.bfloat16),
        scratch_shapes=[WIDE, WIDE, WIDE, GAIN, GAIN, PLACES, pltpu.SemaphoreType.DMA((6,))],
        compiler_params=PARAMS,
        name="exchange_blocks",
    )(queries, keys, values, gain_q.reshape(1, WIDTH), gain_k.reshape(1, WIDTH), positions)


def pick_kernel(place_ref, scattered_ref, out_ref):
    out_ref[...] = scattered_ref[place_ref[0, 0]]


def pick(place, scattered):
    return pl.pallas_call(
        pick_kernel,
        in_specs=[VMEM, VMEM],
        out_specs=VMEM,
        out_shape=jax.ShapeDtypeStruct((2, HEADS * PAIR), jnp.bfloat16),
        compiler_params=PARAMS,
        name="pick_reference",
    )(place, scattered)


def insert_kernel(place_ref, own_ref, other_ref, blocks_ref, out_ref):
    for index in range(REF_ROW // QUARTER):
        out_ref[:, index, :, :] = blocks_ref[:, QUARTER * index : QUARTER * (index + 1), :]

    def put(source_ref):
        for peer, _, whole, shared in peers():
            columns = (2 * whole, 2 * whole + 1, 2 * shared, 2 * shared + 1)
            for part, column in enumerate(columns):
                index, row = REF_ROW // QUARTER + part // 2, 2 * (part % 2)
                out_ref[peer, index, row : row + 2, :] = source_ref[:, lanes(column)]

    other = place_ref[0, 1] == 1

    @pl.when(other)
    def _():
        put(other_ref)

    @pl.when(jnp.logical_not(other))
    def _():
        put(own_ref)


def insert(place, own, other, blocks):
    return pl.pallas_call(
        insert_kernel,
        in_specs=[VMEM] * 4,
        out_specs=VMEM,
        out_shape=jax.ShapeDtypeStruct((PEERS, ALL_SETS, QUARTER, HEAD_DIM), jnp.bfloat16),
        compiler_params=PARAMS,
        name="insert_reference",
    )(place, own, other, blocks)


def flatten_kernel(got_ref, out_ref):
    for peer in range(PEERS):
        for part in range(4):
            target = 2 * PEERS * part + 2 * peer
            index, row = REF_ROW // QUARTER + part // 2, 2 * (part % 2)
            out_ref[0, target : target + 2, :] = got_ref[peer, index, row : row + 2, :]
    for copy in range(1, COLUMN):
        out_ref[copy] = out_ref[0]


def flatten(got):
    return pl.pallas_call(
        flatten_kernel,
        in_specs=[VMEM],
        out_specs=VMEM,
        out_shape=jax.ShapeDtypeStruct((COLUMN, 8 * PEERS, HEAD_DIM), jnp.bfloat16),
        compiler_params=PARAMS,
        name="flatten_reference",
    )(got)


def compact_kernel(got_ref, out_ref):
    for peer in range(PEERS):
        for part in range(2):
            target = PEERS * QUARTER * part + QUARTER * peer
            out_ref[target : target + QUARTER, :] = got_ref[peer, SHARED_ROW // QUARTER + part]


def compact(got):
    return pl.pallas_call(
        compact_kernel,
        in_specs=[VMEM],
        out_specs=VMEM,
        out_shape=jax.ShapeDtypeStruct((2 * PEERS * QUARTER, HEAD_DIM), jnp.bfloat16),
        compiler_params=PARAMS,
        name="shared_head",
    )(got)


def attend_kernel(got_ref, fifth_ref, ref_ref, out_ref, shared_q):
    exponent_scale = HEAD_DIM ** (-0.5) * 1.4426950408889634

    def scores(queried, keyed):
        return lax.dot_general(
            queried, keyed, (((1,), (1,)), ((), ())), preferred_element_type=jnp.float32
        )

    def attention(queried, key_a, value_a, key_b, value_b):
        scores_a = scores(queried, key_a)
        scores_b = scores(queried, key_b)
        largest = jnp.maximum(
            jnp.max(scores_a, axis=1, keepdims=True), jnp.max(scores_b, axis=1, keepdims=True)
        )
        weights_a = jnp.exp2((scores_a - largest) * exponent_scale)
        weights_b = jnp.exp2((scores_b - largest) * exponent_scale)
        total = jnp.sum(weights_a, axis=1, keepdims=True) + jnp.sum(
            weights_b, axis=1, keepdims=True
        )
        mixed = jnp.dot(
            weights_a.astype(jnp.bfloat16), value_a, preferred_element_type=jnp.float32
        ) + jnp.dot(weights_b.astype(jnp.bfloat16), value_b, preferred_element_type=jnp.float32)
        return (mixed / total).astype(jnp.bfloat16)

    def part(source_ref, index, height):
        return source_ref[:, height * index : height * (index + 1), :].reshape(-1, HEAD_DIM)

    def own(index):
        sets = TOKENS // QUARTER
        return got_ref[:, sets * index : sets * (index + 1), :, :].reshape(-1, HEAD_DIM)

    key_own, value_own = own(0), own(1)
    key_ref, value_ref = part(ref_ref, 0, 64), part(ref_ref, 1, 64)
    out_ref[:, 0:TOKENS, :] = attention(own(2), key_own, value_own, key_ref, value_ref).reshape(
        PEERS, TOKENS, HEAD_DIM
    )
    for peer in range(PEERS):
        shared_q[QUARTER * peer : QUARTER * (peer + 1), :] = got_ref[
            peer, SHARED_ROW // QUARTER + 2
        ]
    shared = attention(
        shared_q[...],
        part(fifth_ref, 0, 128),
        part(fifth_ref, 1, 128),
        part(ref_ref, 2, 64),
        part(ref_ref, 3, 64),
    )
    for peer in range(PEERS):
        out_ref[peer, TOKENS : TOKENS + QUARTER, :] = shared[
            QUARTER * peer : QUARTER * (peer + 1), :
        ]


def attend(got, fifth, ref):
    return pl.pallas_call(
        attend_kernel,
        in_specs=[VMEM] * 3,
        out_specs=VMEM,
        out_shape=jax.ShapeDtypeStruct((PEERS, ROWS, HEAD_DIM), jnp.bfloat16),
        scratch_shapes=[pltpu.VMEM((PEERS * QUARTER, HEAD_DIM), jnp.bfloat16)],
        compiler_params=PARAMS,
        name="attention",
    )(got, fifth, ref)


def assemble_kernel(got_ref, out_hbm, whole_ref, sem):
    for peer, blk, whole, shared in peers():
        whole_ref[:, lanes(whole)] = got_ref[peer, 0:TOKENS, :]
        whole_ref[QUARTER * blk : QUARTER * (blk + 1), lanes(shared)] = got_ref[
            peer, TOKENS : TOKENS + QUARTER, :
        ]
    copy = pltpu.make_async_copy(whole_ref, out_hbm, sem)
    copy.start()
    copy.wait()


def assemble(got):
    return pl.pallas_call(
        assemble_kernel,
        in_specs=[VMEM],
        out_specs=HBM,
        out_shape=jax.ShapeDtypeStruct((TOKENS, WIDTH), jnp.bfloat16),
        scratch_shapes=[pltpu.VMEM((TOKENS, WIDTH), jnp.bfloat16), pltpu.SemaphoreType.DMA],
        compiler_params=PARAMS,
        name="assemble",
    )(got)


def local(queries, keys, values, gain_q, gain_k, positions, ref_group):
    pieces, place = make_pieces(keys, values, gain_k, positions, ref_group)
    own = pick(place, lax.all_to_all(pieces, ("x", "core"), 0, 0, tiled=True))
    swap = [
        (half * ULY + uly, (1 - half) * ULY + (uly + ULY // 2) % ULY)
        for half in range(2)
        for uly in range(ULY)
    ]
    other = lax.ppermute(own, ("half", "uly"), swap)
    blocks = make_blocks(queries, keys, values, gain_q, gain_k, positions)
    packed = insert(place, own, other, blocks)
    got = lax.all_to_all(packed, ("blk", "uly"), 0, 0, tiled=True)

    ref = lax.all_to_all(flatten(got), ("x", "core"), 0, 0, tiled=True)
    fifth = lax.all_gather(compact(got), "blk", axis=0, tiled=False)

    attended = attend(got, fifth, ref)
    return assemble(lax.all_to_all(attended, ("blk", "uly"), 0, 0, tiled=True))


def solution(mesh):
    rows = ("x", "half", "core", "blk", "uly")
    fine = Mesh(mesh.devices.reshape(4, 2, 2, BLK, ULY), rows)
    whole, split = P(), P(rows, None)
    in_specs = (split, split, split, whole, whole, P(None, rows), whole)
    return jax.shard_map(local, mesh=fine, in_specs=in_specs, out_specs=split, check_vma=False)
```

time: 394 us -> 110 us (0.28)
  the two profiles are of different devices: /device:TPU:24 before, /device:TPU:6 now
where the time goes in v1:
time: 110 us
  blocking collectives  86.6 us (79%)
  starting transfers between devices  14 us (13%)
  Pallas kernels  7.26 us (7%)
  waiting for transfers between devices  1.69 us (2%)
    all_to_all x1, blocking collectives, local(): got = lax.all_to_all(packed, ('blk', 'uly'), 0, 0, tiled=True)  39.3 us
    all_to_all x1, blocking collectives, local(): return assemble(lax.all_to_all(attended, ('blk', 'uly'), 0, 0, tiled=True))  19.4 us
    all_to_all x1, blocking collectives, local(): own = pick(place, lax.all_to_all(pieces, ('x', 'core'), 0, 0, tiled=True))  15.5 us
    all_gather x1, blocking collectives, local(): fifth = lax.all_gather(compact(got), 'blk', axis=0, tiled=False)  12.4 us
    ppermute x1, starting transfers between devices, local(): other = lax.ppermute(own, ('half', 'uly'), swap)  8.46 us
    all_to_all x1, starting transfers between devices, local(): ref = lax.all_to_all(flatten(got), ('x', 'core'), 0, 0, tiled=True)  5.5 us
  transfers between devices with their start and end apart: 2, of which 1 were waited for; matrix products, arithmetic and copies ran while one was open for 0% of the time, Pallas kernels for 2%

profile of v1, /device:TPU:6, one launch (start us, length us, event | category | flops | bytes accessed | tf_op | source)
XLA Modules:
  0.0 109.7 jit_solution(13868661851721219901)
XLA Ops:
  0.0 2.2 %reference_pieces.1 = (bf16[8,2,10240]{2,1,0:T(2,128)(2,1)}, s32[8,128]{1,0:T(8,128)}) custom-call(bf16[16,5120]{1,0:T(8,128)(2,1)} %k_hbm.3, bf16[16,5120]{1,0:T(8,128)(2,1)} %v_hbm.3, f32[1,5120]{1,0:T(1,128)} %bitcast.5, s32[3,16]{1,0:T(4,128)} %pos_hbm.3, s32[1,16]{1,0:T(1,128)} %bitcast.8), custom_call_target="tpu_custom_call" | custom-call | tf_op jit(solution)/shard_map/reference_pieces/pallas_call | solution.py:143
  2.2 0.0 copy-start.5
  2.2 0.0 copy-start.2
  2.2 15.5 %all_to_all.20.scattered_ref = bf16[8,2,10240]{2,1,0:T(2,128)(2,1)S(1)} all-to-all(bf16[8,2,10240]{2,1,0:T(2,128)(2,1)} %get-tuple-element.8), channel_id=1, replica_groups=mesh['x'=4,'half'=2,'core'=2,'blk'=4,'uly'=8] {'x','core'}, dimensions={0} | all-to-all | bytes 655360 | tf_op jit(solution)/shard_map/all_to_all | solution.py:380
  17.7 0.0 copy-start.4
  17.8 0.0 copy-start.6
  17.8 8.5 %collective-permute-start = (bf16[2,10240]{1,0:T(2,128)(2,1)S(1)}, bf16[2,10240]{1,0:T(2,128)(2,1)S(1)}, u32[]{:S(2)}, u32[]{:S(2)}) collective-permute-start(bf16[2,10240]{1,0:T(2,128)(2,1)S(1)} %pick_reference.1.own_ref), channel_id=1, source_target_pairs={{0,68},{1,69},{2,70},{3,71},{4,64},{5,65},{6,66},{7,67},{64,4},{65... | collective-permute-start | bytes 122888 | tf_op jit(solution)/shard_map/ppermute | solution.py:386
  26.3 0.0 copy-done.2
  26.3 0.0 copy-done
  26.3 0.0 copy-done.1
  26.3 0.0 copy-done.3
  26.3 0.0 copy-done.4
  26.3 0.0 copy-done.6
  26.3 1.7 %exchange_blocks.1.blocks_ref = bf16[32,64,128]{2,1,0:T(8,128)(2,1)S(1)} custom-call(bf16[16,5120]{1,0:T(8,128)(2,1)S(1)} %copy-done.2, bf16[16,5120]{1,0:T(8,128)(2,1)S(1)} %copy-done, bf16[16,5120]{1,0:T(8,128)(2,1)S(1)} %copy-done.1, f32[1,5120]{1,0:T(1,128)S(1)} %bitcast.7, f32[1,5120]{1,0:T(1,128)S(1)} %bitcast.6, s32[3,16]{1,0:T(4,128)S(1)} %copy-done.6), custom_call_target="tpu_custom_call" | custom-call | tf_op jit(solution)/shard_map/exchange_blocks/pallas_call | solution.py:192
  28.0 1.7 %collective-permute-done.other_ref = bf16[2,10240]{1,0:T(2,128)(2,1)S(1)} collective-permute-done((bf16[2,10240]{1,0:T(2,128)(2,1)S(1)}, bf16[2,10240]{1,0:T(2,128)(2,1)S(1)}, u32[]{:S(2)}, u32[]{:S(2)}) %collective-permute-start) | collective-permute-done | bytes 40992 | tf_op jit(solution)/shard_map/ppermute | solution.py:386
  29.7 0.4 insert_reference.1
  30.1 39.3 %all_to_all.21.got_ref = bf16[32,17,4,128]{3,2,1,0:T(4,128)(2,1)S(1)} all-to-all(bf16[32,17,4,128]{3,2,1,0:T(4,128)(2,1)S(1)} %insert_reference.1), channel_id=1, replica_groups=mesh['x'=4,'half'=2,'core'=2,'blk'=4,'uly'=8] {'blk','uly'}, dimensions={0} | all-to-all | bytes 1114112 | tf_op jit(solution)/shard_map/all_to_all | solution.py:389
  69.4 0.9 flatten_reference.1
  70.4 5.5 %all-to-all-start.2 = ((bf16[8,256,128]{2,1,0:T(8,128)(2,1)}), bf16[8,256,128]{2,1,0:T(8,128)(2,1)S(1)}, u32[]{:S(2)}, u32[]{:S(2)}) async-start(bf16[8,256,128]{2,1,0:T(8,128)(2,1)} %flatten_reference.1), calls=%async_computation.2 | async-start | bytes 1048576 | tf_op jit(solution)/shard_map/all_to_all | solution.py:391
  75.9 12.4 %all-gather = bf16[1024,128]{1,0:T(8,128)(2,1)S(1)} all-gather(bf16[256,128]{1,0:T(8,128)(2,1)S(1)} %shared_head.1), channel_id=2, replica_groups=mesh['x'=4,'half'=2,'core'=2,'blk'=4,'uly'=8] {'blk'}, dimensions={0}, use_global_device_ids=true | all-gather | bytes 327680 | tf_op jit(solution)/shard_map/all_gather | solution.py:392
  88.3 0.0 all-to-all-done.2.ref_ref
  88.3 1.3 %attention.1 = bf16[32,24,128]{2,1,0:T(8,128)(2,1)S(1)} custom-call(bf16[32,17,4,128]{3,2,1,0:T(4,128)(2,1)S(1)} %all_to_all.21.got_ref, bf16[4,256,128]{2,1,0:T(8,128)(2,1)S(1)} %bitcast.4, bf16[8,256,128]{2,1,0:T(8,128)(2,1)S(1)} %all-to-all-done.2.ref_ref), custom_call_target="tpu_custom_call" | custom-call | tf_op jit(solution)/shard_map/attention/pallas_call | solution.py:344
  89.7 19.4 %all_to_all.22.got_ref = bf16[32,24,128]{2,1,0:T(8,128)(2,1)S(1)} all-to-all(bf16[32,24,128]{2,1,0:T(8,128)(2,1)S(1)} %attention.1), channel_id=1, replica_groups=mesh['x'=4,'half'=2,'core'=2,'blk'=4,'uly'=8] {'blk','uly'}, dimensions={0} | all-to-all | bytes 393216 | tf_op jit(solution)/shard_map/all_to_all | solution.py:395
  109.0 0.7 assemble.1
  (6 shorter events, 0.1 us)
Async XLA Ops:
  2.2 15.5 %copy-start.5 = (s32[8,128]{1,0:T(8,128)S(1)}, s32[8,128]{1,0:T(8,128)}, u32[]{:S(2)}) copy-start(s32[8,128]{1,0:T(8,128)} %get-tuple-element.7.place_ref) | copy-start | bytes 12292
  2.2 24.1 %copy-start.2 = (bf16[16,5120]{1,0:T(8,128)(2,1)S(1)}, bf16[16,5120]{1,0:T(8,128)(2,1)}, u32[]{:S(2)}) copy-start(bf16[16,5120]{1,0:T(8,128)(2,1)} %q_hbm.1) | copy-start | bytes 491524
  17.7 8.6 %copy-start = (bf16[16,5120]{1,0:T(8,128)(2,1)S(1)}, bf16[16,5120]{1,0:T(8,128)(2,1)}, u32[]{:S(2)}) copy-start(bf16[16,5120]{1,0:T(8,128)(2,1)} %k_hbm.3) | copy-start | bytes 491524
  17.7 8.6 %copy-start.1 = (bf16[16,5120]{1,0:T(8,128)(2,1)S(1)}, bf16[16,5120]{1,0:T(8,128)(2,1)}, u32[]{:S(2)}) copy-start(bf16[16,5120]{1,0:T(8,128)(2,1)} %v_hbm.3) | copy-start | bytes 491524
  17.7 8.6 %copy-start.3 = (f32[5120]{0:T(1024)S(1)}, f32[5120]{0:T(1024)}, u32[]{:S(2)}) copy-start(f32[5120]{0:T(1024)} %param.11) | copy-start | bytes 61444
  17.7 8.6 %copy-start.4 = (f32[5120]{0:T(1024)S(1)}, f32[5120]{0:T(1024)}, u32[]{:S(2)}) copy-start(f32[5120]{0:T(1024)} %param.10) | copy-start | bytes 61444
  17.8 8.6 %copy-start.6 = (s32[3,16]{1,0:T(4,128)S(1)}, s32[3,16]{1,0:T(4,128)}, u32[]{:S(2)}) copy-start(s32[3,16]{1,0:T(4,128)} %pos_hbm.3) | copy-start | bytes 580
  17.8 11.9 %collective-permute-start = (bf16[2,10240]{1,0:T(2,128)(2,1)S(1)}, bf16[2,10240]{1,0:T(2,128)(2,1)S(1)}, u32[]{:S(2)}, u32[]{:S(2)}) collective-permute-start(bf16[2,10240]{1,0:T(2,128)(2,1)S(1)} %pick_reference.1.own_ref), channel_id=1, source_target_pairs={{0,68},{1,69},{2,70},{3,71},{4,64},{5,65},{6,66},{7,67},{64,4},{65... | collective-permute-start | bytes 122888 | tf_op jit(solution)/shard_map/ppermute | solution.py:386
  70.4 18.0 %all-to-all-start.2 = ((bf16[8,256,128]{2,1,0:T(8,128)(2,1)}), bf16[8,256,128]{2,1,0:T(8,128)(2,1)S(1)}, u32[]{:S(2)}, u32[]{:S(2)}) async-start(bf16[8,256,128]{2,1,0:T(8,128)(2,1)} %flatten_reference.1), calls=%async_computation.2 | async-start | bytes 1048576 | tf_op jit(solution)/shard_map/all_to_all | solution.py:391

commit v2 on v1

--- a/solution.py
+++ b/solution.py
@@ -248,22 +248,27 @@
     )(place, own, other, blocks)
 
 
-def flatten_kernel(got_ref, out_ref):
+def flatten_kernel(got_ref, out_hbm, flat_ref, sems):
     for peer in range(PEERS):
         for part in range(4):
             target = 2 * PEERS * part + 2 * peer
             index, row = REF_ROW // QUARTER + part // 2, 2 * (part % 2)
-            out_ref[0, target : target + 2, :] = got_ref[peer, index, row : row + 2, :]
-    for copy in range(1, COLUMN):
-        out_ref[copy] = out_ref[0]
+            flat_ref[target : target + 2, :] = got_ref[peer, index, row : row + 2, :]
+    copies = start_all([(flat_ref, out_hbm.at[copy]) for copy in range(COLUMN)], sems)
+    for copy in copies:
+        copy.wait()
 
 
 def flatten(got):
     return pl.pallas_call(
         flatten_kernel,
         in_specs=[VMEM],
-        out_specs=VMEM,
+        out_specs=HBM,
         out_shape=jax.ShapeDtypeStruct((COLUMN, 8 * PEERS, HEAD_DIM), jnp.bfloat16),
+        scratch_shapes=[
+            pltpu.VMEM((8 * PEERS, HEAD_DIM), jnp.bfloat16),
+            pltpu.SemaphoreType.DMA((COLUMN,)),
+        ],
         compiler_params=PARAMS,
         name="flatten_reference",
     )(got)
@@ -320,8 +325,9 @@
 
     key_own, value_own = own(0), own(1)
     key_ref, value_ref = part(ref_ref, 0, 64), part(ref_ref, 1, 64)
-    out_ref[:, 0:TOKENS, :] = attention(own(2), key_own, value_own, key_ref, value_ref).reshape(
-        PEERS, TOKENS, HEAD_DIM
+    sets = TOKENS // QUARTER
+    out_ref[:, 0:sets, :, :] = attention(own(2), key_own, value_own, key_ref, value_ref).reshape(
+        PEERS, sets, QUARTER, HEAD_DIM
     )
     for peer in range(PEERS):
         shared_q[QUARTER * peer : QUARTER * (peer + 1), :] = got_ref[
@@ -335,9 +341,7 @@
         part(ref_ref, 3, 64),
     )
     for peer in range(PEERS):
-        out_ref[peer, TOKENS : TOKENS + QUARTER, :] = shared[
-            QUARTER * peer : QUARTER * (peer + 1), :
-        ]
+        out_ref[peer, sets, :, :] = shared[QUARTER * peer : QUARTER * (peer + 1), :]
 
 
 def attend(got, fifth, ref):
@@ -345,7 +349,7 @@
         attend_kernel,
         in_specs=[VMEM] * 3,
         out_specs=VMEM,
-        out_shape=jax.ShapeDtypeStruct((PEERS, ROWS, HEAD_DIM), jnp.bfloat16),
+        out_shape=jax.ShapeDtypeStruct((PEERS, TOKENS // QUARTER + 1, QUARTER, HEAD_DIM), jnp.bfloat16),
         scratch_shapes=[pltpu.VMEM((PEERS * QUARTER, HEAD_DIM), jnp.bfloat16)],
         compiler_params=PARAMS,
         name="attention",
@@ -354,10 +358,9 @@
 
 def assemble_kernel(got_ref, out_hbm, whole_ref, sem):
     for peer, blk, whole, shared in peers():
-        whole_ref[:, lanes(whole)] = got_ref[peer, 0:TOKENS, :]
-        whole_ref[QUARTER * blk : QUARTER * (blk + 1), lanes(shared)] = got_ref[
-            peer, TOKENS : TOKENS + QUARTER, :
-        ]
+        sets = TOKENS // QUARTER
+        whole_ref[:, lanes(whole)] = got_ref[peer, 0:sets].reshape(TOKENS, HEAD_DIM)
+        whole_ref[QUARTER * blk : QUARTER * (blk + 1), lanes(shared)] = got_ref[peer, sets]
     copy = pltpu.make_async_copy(whole_ref, out_hbm, sem)
     copy.start()
     copy.wait()

time: 110 us -> 108 us (0.982)
  the two profiles are of different devices: /device:TPU:6 before, /device:TPU:24 now
where the time goes in v2:
time: 108 us; the launch traced here: 106 us
  blocking collectives  80.9 us (75%)
  starting transfers between devices  16.4 us (15%)
  Pallas kernels  7.3 us (7%)
  waiting for transfers between devices  1.69 us (2%)
    all_to_all x1, blocking collectives, local(): got = lax.all_to_all(packed, ('blk', 'uly'), 0, 0, tiled=True)  37.1 us
    all_to_all x1, blocking collectives, local(): return assemble(lax.all_to_all(attended, ('blk', 'uly'), 0, 0, tiled=True))  18.8 us
    ppermute x1, starting transfers between devices, local(): other = lax.ppermute(own, ('half', 'uly'), swap)  12.9 us
    all_to_all x1, blocking collectives, local(): own = pick(place, lax.all_to_all(pieces, ('x', 'core'), 0, 0, tiled=True))  12.7 us
    all_gather x1, blocking collectives, local(): fifth = lax.all_gather(compact(got), 'blk', axis=0, tiled=False)  12.3 us
    all_to_all x1, starting transfers between devices, local(): ref = lax.all_to_all(flatten(got), ('x', 'core'), 0, 0, tiled=True)  3.5 us
    pallas_call x1, Pallas kernels, make_pieces(): pl.pallas_call(pieces_kernel, in_specs=[HBM] * 5, out_specs=(VMEM,) * 2,...  2.2 us
  transfers between devices with their start and end apart: 2, of which 1 were waited for; matrix products, arithmetic and copies ran while one was open for 0% of the time, Pallas kernels for 2%

profile of v2, /device:TPU:24, one launch (start us, length us, event | category | flops | bytes accessed | tf_op | source)
XLA Modules:
  0.0 106.4 jit_solution(15403590444788533314)
XLA Ops:
  0.0 2.2 %reference_pieces.1 = (bf16[8,2,10240]{2,1,0:T(2,128)(2,1)}, s32[8,128]{1,0:T(8,128)}) custom-call(bf16[16,5120]{1,0:T(8,128)(2,1)} %k_hbm.3, bf16[16,5120]{1,0:T(8,128)(2,1)} %v_hbm.3, f32[1,5120]{1,0:T(1,128)} %bitcast.5, s32[3,16]{1,0:T(4,128)} %pos_hbm.3, s32[1,16]{1,0:T(1,128)} %bitcast.8), custom_call_target="tpu_custom_call" | custom-call | tf_op jit(solution)/shard_map/reference_pieces/pallas_call | solution.py:143
  2.2 0.0 copy-start.5
  2.2 0.0 copy-start.2
  2.2 12.7 %all_to_all.20.scattered_ref = bf16[8,2,10240]{2,1,0:T(2,128)(2,1)S(1)} all-to-all(bf16[8,2,10240]{2,1,0:T(2,128)(2,1)} %get-tuple-element.8), channel_id=1, replica_groups=mesh['x'=4,'half'=2,'core'=2,'blk'=4,'uly'=8] {'x','core'}, dimensions={0} | all-to-all | bytes 655360 | tf_op jit(solution)/shard_map/all_to_all | solution.py:383
  14.9 0.0 copy-done.5
  14.9 0.0 copy-start.4
  14.9 0.0 copy-start.6
  15.0 12.9 %collective-permute-start = (bf16[2,10240]{1,0:T(2,128)(2,1)S(1)}, bf16[2,10240]{1,0:T(2,128)(2,1)S(1)}, u32[]{:S(2)}, u32[]{:S(2)}) collective-permute-start(bf16[2,10240]{1,0:T(2,128)(2,1)S(1)} %pick_reference.1.own_ref), channel_id=1, source_target_pairs={{0,68},{1,69},{2,70},{3,71},{4,64},{5,65},{6,66},{7,67},{64,4},{65... | collective-permute-start | bytes 122888 | tf_op jit(solution)/shard_map/ppermute | solution.py:389
  27.9 0.0 copy-done.2
  27.9 0.0 copy-done
  27.9 0.0 copy-done.1
  27.9 0.0 copy-done.3
  27.9 0.0 copy-done.4
  27.9 1.7 %exchange_blocks.1.blocks_ref = bf16[32,64,128]{2,1,0:T(8,128)(2,1)S(1)} custom-call(bf16[16,5120]{1,0:T(8,128)(2,1)S(1)} %copy-done.2, bf16[16,5120]{1,0:T(8,128)(2,1)S(1)} %copy-done, bf16[16,5120]{1,0:T(8,128)(2,1)S(1)} %copy-done.1, f32[1,5120]{1,0:T(1,128)S(1)} %bitcast.7, f32[1,5120]{1,0:T(1,128)S(1)} %bitcast.6, s32[3,16]{1,0:T(4,128)S(1)} %copy-done.6), custom_call_target="tpu_custom_call" | custom-call | tf_op jit(solution)/shard_map/exchange_blocks/pallas_call | solution.py:192
  29.6 1.7 %collective-permute-done.other_ref = bf16[2,10240]{1,0:T(2,128)(2,1)S(1)} collective-permute-done((bf16[2,10240]{1,0:T(2,128)(2,1)S(1)}, bf16[2,10240]{1,0:T(2,128)(2,1)S(1)}, u32[]{:S(2)}, u32[]{:S(2)}) %collective-permute-start) | collective-permute-done | bytes 40992 | tf_op jit(solution)/shard_map/ppermute | solution.py:389
  31.3 0.4 insert_reference.1
  31.7 37.1 %all_to_all.21.got_ref = bf16[32,17,4,128]{3,2,1,0:T(4,128)(2,1)S(1)} all-to-all(bf16[32,17,4,128]{3,2,1,0:T(4,128)(2,1)S(1)} %insert_reference.1), channel_id=1, replica_groups=mesh['x'=4,'half'=2,'core'=2,'blk'=4,'uly'=8] {'blk','uly'}, dimensions={0} | all-to-all | bytes 1114112 | tf_op jit(solution)/shard_map/all_to_all | solution.py:392
  68.8 0.9 flatten_reference.1
  69.8 3.5 %all-to-all-start.2 = ((bf16[8,256,128]{2,1,0:T(8,128)(2,1)}), bf16[8,256,128]{2,1,0:T(8,128)(2,1)S(1)}, u32[]{:S(2)}, u32[]{:S(2)}) async-start(bf16[8,256,128]{2,1,0:T(8,128)(2,1)} %flatten_reference.1), calls=%async_computation.2 | async-start | bytes 1048576 | tf_op jit(solution)/shard_map/all_to_all | solution.py:394
  73.3 12.3 %all-gather = bf16[1024,128]{1,0:T(8,128)(2,1)S(1)} all-gather(bf16[256,128]{1,0:T(8,128)(2,1)S(1)} %shared_head.1), channel_id=2, replica_groups=mesh['x'=4,'half'=2,'core'=2,'blk'=4,'uly'=8] {'blk'}, dimensions={0}, use_global_device_ids=true | all-gather | bytes 327680 | tf_op jit(solution)/shard_map/all_gather | solution.py:395
  85.6 0.0 all-to-all-done.2.ref_ref
  85.6 1.3 %attention.1 = bf16[32,5,4,128]{3,2,1,0:T(4,128)(2,1)S(1)} custom-call(bf16[32,17,4,128]{3,2,1,0:T(4,128)(2,1)S(1)} %all_to_all.21.got_ref, bf16[4,256,128]{2,1,0:T(8,128)(2,1)S(1)} %bitcast.4, bf16[8,256,128]{2,1,0:T(8,128)(2,1)S(1)} %all-to-all-done.2.ref_ref), custom_call_target="tpu_custom_call" | custom-call | tf_op jit(solution)/shard_map/attention/pallas_call | solution.py:348
  86.9 18.8 %all_to_all.22.got_ref = bf16[32,5,4,128]{3,2,1,0:T(4,128)(2,1)S(1)} all-to-all(bf16[32,5,4,128]{3,2,1,0:T(4,128)(2,1)S(1)} %attention.1), channel_id=1, replica_groups=mesh['x'=4,'half'=2,'core'=2,'blk'=4,'uly'=8] {'blk','uly'}, dimensions={0} | all-to-all | bytes 327680 | tf_op jit(solution)/shard_map/all_to_all | solution.py:398
  105.7 0.7 assemble.1
  (6 shorter events, 0.1 us)
Async XLA Ops:
  2.2 12.7 %copy-start.5 = (s32[8,128]{1,0:T(8,128)S(1)}, s32[8,128]{1,0:T(8,128)}, u32[]{:S(2)}) copy-start(s32[8,128]{1,0:T(8,128)} %get-tuple-element.7.place_ref) | copy-start | bytes 12292
  2.2 25.7 %copy-start.2 = (bf16[16,5120]{1,0:T(8,128)(2,1)S(1)}, bf16[16,5120]{1,0:T(8,128)(2,1)}, u32[]{:S(2)}) copy-start(bf16[16,5120]{1,0:T(8,128)(2,1)} %q_hbm.1) | copy-start | bytes 491524
  14.9 13.0 %copy-start = (bf16[16,5120]{1,0:T(8,128)(2,1)S(1)}, bf16[16,5120]{1,0:T(8,128)(2,1)}, u32[]{:S(2)}) copy-start(bf16[16,5120]{1,0:T(8,128)(2,1)} %k_hbm.3) | copy-start | bytes 491524
  14.9 13.0 %copy-start.1 = (bf16[16,5120]{1,0:T(8,128)(2,1)S(1)}, bf16[16,5120]{1,0:T(8,128)(2,1)}, u32[]{:S(2)}) copy-start(bf16[16,5120]{1,0:T(8,128)(2,1)} %v_hbm.3) | copy-start | bytes 491524
  14.9 13.0 %copy-start.3 = (f32[5120]{0:T(1024)S(1)}, f32[5120]{0:T(1024)}, u32[]{:S(2)}) copy-start(f32[5120]{0:T(1024)} %param.11) | copy-start | bytes 61444
  14.9 13.0 %copy-start.4 = (f32[5120]{0:T(1024)S(1)}, f32[5120]{0:T(1024)}, u32[]{:S(2)}) copy-start(f32[5120]{0:T(1024)} %param.10) | copy-start | bytes 61444
  14.9 13.0 %copy-start.6 = (s32[3,16]{1,0:T(4,128)S(1)}, s32[3,16]{1,0:T(4,128)}, u32[]{:S(2)}) copy-start(s32[3,16]{1,0:T(4,128)} %pos_hbm.3) | copy-start | bytes 580
  15.0 16.3 %collective-permute-start = (bf16[2,10240]{1,0:T(2,128)(2,1)S(1)}, bf16[2,10240]{1,0:T(2,128)(2,1)S(1)}, u32[]{:S(2)}, u32[]{:S(2)}) collective-permute-start(bf16[2,10240]{1,0:T(2,128)(2,1)S(1)} %pick_reference.1.own_ref), channel_id=1, source_target_pairs={{0,68},{1,69},{2,70},{3,71},{4,64},{5,65},{6,66},{7,67},{64,4},{65... | collective-permute-start | bytes 122888 | tf_op jit(solution)/shard_map/ppermute | solution.py:389
  69.8 15.8 %all-to-all-start.2 = ((bf16[8,256,128]{2,1,0:T(8,128)(2,1)}), bf16[8,256,128]{2,1,0:T(8,128)(2,1)S(1)}, u32[]{:S(2)}, u32[]{:S(2)}) async-start(bf16[8,256,128]{2,1,0:T(8,128)(2,1)} %flatten_reference.1), calls=%async_computation.2 | async-start | bytes 1048576 | tf_op jit(solution)/shard_map/all_to_all | solution.py:394

commit v3 on v2

--- a/solution.py
+++ b/solution.py
@@ -356,14 +356,23 @@
     )(got, fifth, ref)
 
 
-def assemble_kernel(got_ref, out_hbm, whole_ref, sem):
-    for peer, blk, whole, shared in peers():
-        sets = TOKENS // QUARTER
-        whole_ref[:, lanes(whole)] = got_ref[peer, 0:sets].reshape(TOKENS, HEAD_DIM)
-        whole_ref[QUARTER * blk : QUARTER * (blk + 1), lanes(shared)] = got_ref[peer, sets]
-    copy = pltpu.make_async_copy(whole_ref, out_hbm, sem)
-    copy.start()
-    copy.wait()
+def assemble_kernel(got_ref, out_hbm, whole_ref, sems):
+    sets = TOKENS // QUARTER
+    span = WIDTH // 2
+    copies = []
+    for half in range(2):
+        for peer, blk, whole, shared in peers():
+            if whole * HEAD_DIM // span == half:
+                whole_ref[:, lanes(whole)] = got_ref[peer, 0:sets].reshape(TOKENS, HEAD_DIM)
+            if shared * HEAD_DIM // span == half:
+                whole_ref[QUARTER * blk : QUARTER * (blk + 1), lanes(shared)] = got_ref[peer, sets]
+        where = lanes(half, span)
+        copies.append(
+            pltpu.make_async_copy(whole_ref.at[:, where], out_hbm.at[:, where], sems.at[half])
+        )
+        copies[half].start()
+    for copy in copies:
+        copy.wait()
 
 
 def assemble(got):
@@ -372,7 +381,7 @@
         in_specs=[VMEM],
         out_specs=HBM,
         out_shape=jax.ShapeDtypeStruct((TOKENS, WIDTH), jnp.bfloat16),
-        scratch_shapes=[pltpu.VMEM((TOKENS, WIDTH), jnp.bfloat16), pltpu.SemaphoreType.DMA],
+        scratch_shapes=[pltpu.VMEM((TOKENS, WIDTH), jnp.bfloat16), pltpu.SemaphoreType.DMA((2,))],
         compiler_params=PARAMS,
         name="assemble",
     )(got)

time: 108 us -> 108 us (level)
  no operation moved by 1% of the time
where the time goes in v3:
time: 108 us; the launch traced here: 106 us
  blocking collectives  80.9 us (75%)
  starting transfers between devices  16.4 us (15%)
  Pallas kernels  7.28 us (7%)
  waiting for transfers between devices  1.69 us (2%)
    all_to_all x1, blocking collectives, local(): got = lax.all_to_all(packed, ('blk', 'uly'), 0, 0, tiled=True)  37.1 us
    all_to_all x1, blocking collectives, local(): return assemble(lax.all_to_all(attended, ('blk', 'uly'), 0, 0, tiled=True))  18.8 us
    ppermute x1, starting transfers between devices, local(): other = lax.ppermute(own, ('half', 'uly'), swap)  12.9 us
    all_to_all x1, blocking collectives, local(): own = pick(place, lax.all_to_all(pieces, ('x', 'core'), 0, 0, tiled=True))  12.7 us
    all_gather x1, blocking collectives, local(): fifth = lax.all_gather(compact(got), 'blk', axis=0, tiled=False)  12.3 us
    all_to_all x1, starting transfers between devices, local(): ref = lax.all_to_all(flatten(got), ('x', 'core'), 0, 0, tiled=True)  3.5 us
    pallas_call x1, Pallas kernels, make_pieces(): pl.pallas_call(pieces_kernel, in_specs=[HBM] * 5, out_specs=(VMEM,) * 2,...  2.2 us
  transfers between devices with their start and end apart: 2, of which 1 were waited for; matrix products, arithmetic and copies ran while one was open for 0% of the time, Pallas kernels for 2%

profile of v3, /device:TPU:24, one launch (start us, length us, event | category | flops | bytes accessed | tf_op | source)
XLA Modules:
  0.0 106.4 jit_solution(16340503362457264957)
XLA Ops:
  0.0 2.2 %reference_pieces.1 = (bf16[8,2,10240]{2,1,0:T(2,128)(2,1)}, s32[8,128]{1,0:T(8,128)}) custom-call(bf16[16,5120]{1,0:T(8,128)(2,1)} %k_hbm.3, bf16[16,5120]{1,0:T(8,128)(2,1)} %v_hbm.3, f32[1,5120]{1,0:T(1,128)} %bitcast.5, s32[3,16]{1,0:T(4,128)} %pos_hbm.3, s32[1,16]{1,0:T(1,128)} %bitcast.8), custom_call_target="tpu_custom_call" | custom-call | tf_op jit(solution)/shard_map/reference_pieces/pallas_call | solution.py:143
  2.2 0.0 copy-start.5
  2.2 0.0 copy-start.2
  2.2 12.7 %all_to_all.20.scattered_ref = bf16[8,2,10240]{2,1,0:T(2,128)(2,1)S(1)} all-to-all(bf16[8,2,10240]{2,1,0:T(2,128)(2,1)} %get-tuple-element.8), channel_id=1, replica_groups=mesh['x'=4,'half'=2,'core'=2,'blk'=4,'uly'=8] {'x','core'}, dimensions={0} | all-to-all | bytes 655360 | tf_op jit(solution)/shard_map/all_to_all | solution.py:392
  14.9 0.0 copy-done.5
  14.9 0.0 copy-start.4
  14.9 0.0 copy-start.6
  15.0 12.9 %collective-permute-start = (bf16[2,10240]{1,0:T(2,128)(2,1)S(1)}, bf16[2,10240]{1,0:T(2,128)(2,1)S(1)}, u32[]{:S(2)}, u32[]{:S(2)}) collective-permute-start(bf16[2,10240]{1,0:T(2,128)(2,1)S(1)} %pick_reference.1.own_ref), channel_id=1, source_target_pairs={{0,68},{1,69},{2,70},{3,71},{4,64},{5,65},{6,66},{7,67},{64,4},{65... | collective-permute-start | bytes 122888 | tf_op jit(solution)/shard_map/ppermute | solution.py:398
  27.9 0.0 copy-done.2
  27.9 0.0 copy-done
  27.9 0.0 copy-done.1
  27.9 0.0 copy-done.3
  27.9 0.0 copy-done.4
  27.9 1.7 %exchange_blocks.1.blocks_ref = bf16[32,64,128]{2,1,0:T(8,128)(2,1)S(1)} custom-call(bf16[16,5120]{1,0:T(8,128)(2,1)S(1)} %copy-done.2, bf16[16,5120]{1,0:T(8,128)(2,1)S(1)} %copy-done, bf16[16,5120]{1,0:T(8,128)(2,1)S(1)} %copy-done.1, f32[1,5120]{1,0:T(1,128)S(1)} %bitcast.7, f32[1,5120]{1,0:T(1,128)S(1)} %bitcast.6, s32[3,16]{1,0:T(4,128)S(1)} %copy-done.6), custom_call_target="tpu_custom_call" | custom-call | tf_op jit(solution)/shard_map/exchange_blocks/pallas_call | solution.py:192
  29.6 1.7 %collective-permute-done.other_ref = bf16[2,10240]{1,0:T(2,128)(2,1)S(1)} collective-permute-done((bf16[2,10240]{1,0:T(2,128)(2,1)S(1)}, bf16[2,10240]{1,0:T(2,128)(2,1)S(1)}, u32[]{:S(2)}, u32[]{:S(2)}) %collective-permute-start) | collective-permute-done | bytes 40992 | tf_op jit(solution)/shard_map/ppermute | solution.py:398
  31.3 0.4 insert_reference.1
  31.7 37.1 %all_to_all.21.got_ref = bf16[32,17,4,128]{3,2,1,0:T(4,128)(2,1)S(1)} all-to-all(bf16[32,17,4,128]{3,2,1,0:T(4,128)(2,1)S(1)} %insert_reference.1), channel_id=1, replica_groups=mesh['x'=4,'half'=2,'core'=2,'blk'=4,'uly'=8] {'blk','uly'}, dimensions={0} | all-to-all | bytes 1114112 | tf_op jit(solution)/shard_map/all_to_all | solution.py:401
  68.8 0.9 flatten_reference.1
  69.8 3.5 %all-to-all-start.2 = ((bf16[8,256,128]{2,1,0:T(8,128)(2,1)}), bf16[8,256,128]{2,1,0:T(8,128)(2,1)S(1)}, u32[]{:S(2)}, u32[]{:S(2)}) async-start(bf16[8,256,128]{2,1,0:T(8,128)(2,1)} %flatten_reference.1), calls=%async_computation.2 | async-start | bytes 1048576 | tf_op jit(solution)/shard_map/all_to_all | solution.py:403
  73.3 12.3 %all-gather = bf16[1024,128]{1,0:T(8,128)(2,1)S(1)} all-gather(bf16[256,128]{1,0:T(8,128)(2,1)S(1)} %shared_head.1), channel_id=2, replica_groups=mesh['x'=4,'half'=2,'core'=2,'blk'=4,'uly'=8] {'blk'}, dimensions={0}, use_global_device_ids=true | all-gather | bytes 327680 | tf_op jit(solution)/shard_map/all_gather | solution.py:404
  85.6 0.0 all-to-all-done.2.ref_ref
  85.6 1.3 %attention.1 = bf16[32,5,4,128]{3,2,1,0:T(4,128)(2,1)S(1)} custom-call(bf16[32,17,4,128]{3,2,1,0:T(4,128)(2,1)S(1)} %all_to_all.21.got_ref, bf16[4,256,128]{2,1,0:T(8,128)(2,1)S(1)} %bitcast.4, bf16[8,256,128]{2,1,0:T(8,128)(2,1)S(1)} %all-to-all-done.2.ref_ref), custom_call_target="tpu_custom_call" | custom-call | tf_op jit(solution)/shard_map/attention/pallas_call | solution.py:348
  86.9 18.8 %all_to_all.22.got_ref = bf16[32,5,4,128]{3,2,1,0:T(4,128)(2,1)S(1)} all-to-all(bf16[32,5,4,128]{3,2,1,0:T(4,128)(2,1)S(1)} %attention.1), channel_id=1, replica_groups=mesh['x'=4,'half'=2,'core'=2,'blk'=4,'uly'=8] {'blk','uly'}, dimensions={0} | all-to-all | bytes 327680 | tf_op jit(solution)/shard_map/all_to_all | solution.py:407
  105.7 0.7 assemble.1
  (6 shorter events, 0.1 us)
Async XLA Ops:
  2.2 12.7 %copy-start.5 = (s32[8,128]{1,0:T(8,128)S(1)}, s32[8,128]{1,0:T(8,128)}, u32[]{:S(2)}) copy-start(s32[8,128]{1,0:T(8,128)} %get-tuple-element.7.place_ref) | copy-start | bytes 12292
  2.2 25.7 %copy-start.2 = (bf16[16,5120]{1,0:T(8,128)(2,1)S(1)}, bf16[16,5120]{1,0:T(8,128)(2,1)}, u32[]{:S(2)}) copy-start(bf16[16,5120]{1,0:T(8,128)(2,1)} %q_hbm.1) | copy-start | bytes 491524
  14.9 13.0 %copy-start = (bf16[16,5120]{1,0:T(8,128)(2,1)S(1)}, bf16[16,5120]{1,0:T(8,128)(2,1)}, u32[]{:S(2)}) copy-start(bf16[16,5120]{1,0:T(8,128)(2,1)} %k_hbm.3) | copy-start | bytes 491524
  14.9 13.0 %copy-start.1 = (bf16[16,5120]{1,0:T(8,128)(2,1)S(1)}, bf16[16,5120]{1,0:T(8,128)(2,1)}, u32[]{:S(2)}) copy-start(bf16[16,5120]{1,0:T(8,128)(2,1)} %v_hbm.3) | copy-start | bytes 491524
  14.9 13.0 %copy-start.3 = (f32[5120]{0:T(1024)S(1)}, f32[5120]{0:T(1024)}, u32[]{:S(2)}) copy-start(f32[5120]{0:T(1024)} %param.11) | copy-start | bytes 61444
  14.9 13.0 %copy-start.4 = (f32[5120]{0:T(1024)S(1)}, f32[5120]{0:T(1024)}, u32[]{:S(2)}) copy-start(f32[5120]{0:T(1024)} %param.10) | copy-start | bytes 61444
  14.9 13.0 %copy-start.6 = (s32[3,16]{1,0:T(4,128)S(1)}, s32[3,16]{1,0:T(4,128)}, u32[]{:S(2)}) copy-start(s32[3,16]{1,0:T(4,128)} %pos_hbm.3) | copy-start | bytes 580
  15.0 16.3 %collective-permute-start = (bf16[2,10240]{1,0:T(2,128)(2,1)S(1)}, bf16[2,10240]{1,0:T(2,128)(2,1)S(1)}, u32[]{:S(2)}, u32[]{:S(2)}) collective-permute-start(bf16[2,10240]{1,0:T(2,128)(2,1)S(1)} %pick_reference.1.own_ref), channel_id=1, source_target_pairs={{0,68},{1,69},{2,70},{3,71},{4,64},{5,65},{6,66},{7,67},{64,4},{65... | collective-permute-start | bytes 122888 | tf_op jit(solution)/shard_map/ppermute | solution.py:398
  69.8 15.8 %all-to-all-start.2 = ((bf16[8,256,128]{2,1,0:T(8,128)(2,1)}), bf16[8,256,128]{2,1,0:T(8,128)(2,1)S(1)}, u32[]{:S(2)}, u32[]{:S(2)}) async-start(bf16[8,256,128]{2,1,0:T(8,128)(2,1)} %flatten_reference.1), calls=%async_computation.2 | async-start | bytes 1048576 | tf_op jit(solution)/shard_map/all_to_all | solution.py:403
